TPU v7x, 32 devices: a whole 2x2x4 slice. The times are simulated.
32 devices in a mesh: phi: 8 (over z, core), mom: 4 (over y, x).
Axes of the slice: x: 2, y: 2, z: 4, core: 2. Of those that a mesh axis runs over, the one named last changes fastest.
Arguments:
- spectra: float32 [32, 4, 16, 64, 256], P('mom', None, 'phi'), may hold values from 0.1 to 3
- production: bfloat16 [32, 32], replicated, may hold values from 0 to 0.119628906
- bin_group: int32 [32], replicated, may hold values from 0 to 3
- parent_of: int32 [4], replicated, may hold values from 0 to 3
- diffusivity: float32 [64, 256], replicated, may hold values from 0.05 to 0.22
- height_inverse: float32 [64, 64], replicated, may hold values from -1 to 1, as said below
- loss_rate: float32 [32], P('mom'), may hold values from 2 to 20
- density: float32 [16, 64, 256], P('phi'), may hold values from 0.5 to 2
Outputs:
- spectra_out: float32 [32, 4, 16, 64, 256], P('mom', None, 'phi')
Inputs may be any that keep to these rules, and one draw needn't show every extreme that they name: `height_inverse`: diagonal entries lie between 0.7 and 1, off-diagonal entries are small.
All inputs are finite; a program needn't handle non-finite values.
Results may differ from a plain program's by a relative error of at most 0.00085.
Values may be sent and summed in bfloat16 or wider, within the bound.
A program may use at most 64 MiB of HBM per device.

v0:
```python
import jax
import jax.numpy as jnp
from jax import lax
from jax.sharding import PartitionSpec as P


def padded_2(cells, sides, width):
    for axis, dim in sides:
        count = lax.axis_size(axis)
        head = lax.slice_in_dim(cells, 0, width, axis=dim)
        tail = lax.slice_in_dim(cells, cells.shape[dim] - width, cells.shape[dim], axis=dim)
        cells = jnp.concatenate(
            [
                lax.ppermute(tail, axis, [(i, (i + 1) % count) for i in range(count)]),
                cells,
                lax.ppermute(head, axis, [((i + 1) % count, i) for i in range(count)]),
            ],
            axis=dim,
        )
    return cells


def passed_along(block, axis, distance):
    devices = range(lax.axis_size(axis))
    route = [(i - distance, i) for i in devices if i - distance in devices]
    return lax.ppermute(block, axis, route)


def one_step(
    state, production, bin_group, parent_of, diffusivity, height_inverse, loss_rate, density
):
    bins_here = state.shape[0]
    species = state.shape[1]
    onehot = (parent_of[:, None] == jnp.arange(species, dtype=jnp.int32)[None, :]).astype(
        jnp.float32
    )
    parents = jnp.einsum("st,qtxzr->qsxzr", onehot, state, precision=lax.Precision.HIGHEST).astype(
        jnp.bfloat16
    )
    same = bin_group[:, None] == bin_group[None, :]
    kernel = jnp.where(same, production, jnp.zeros_like(production))
    first_bin = lax.axis_index("mom") * bins_here
    flat_parents = parents.reshape(bins_here, -1)
    kernel_rows = lax.dynamic_slice_in_dim(kernel, first_bin, bins_here, 0)
    source = jnp.dot(
        kernel_rows,
        lax.all_gather(flat_parents, "mom", axis=0, tiled=True),
        preferred_element_type=jnp.float32,
    )
    sourced = state + source.reshape(state.shape)
    padded = padded_2(sourced.astype(jnp.bfloat16), (("phi", 2),), 1).astype(sourced.dtype)
    lap_phi = padded[:, :, 2:] + padded[:, :, :-2] - 2.0 * sourced
    pad_r = jnp.pad(sourced, ((0, 0), (0, 0), (0, 0), (0, 0), (1, 1)))
    lap_r = pad_r[..., 2:] + pad_r[..., :-2] - 2.0 * sourced
    moved = sourced + diffusivity * lap_phi + 0.5 * diffusivity * lap_r
    pad_z = jnp.pad(moved, ((0, 0), (0, 0), (0, 0), (1, 1), (0, 0)))
    halfway = moved + 0.25 * (pad_z[:, :, :, 2:] + pad_z[:, :, :, :-2] - 2.0 * moved)
    settled = jnp.einsum(
        "yz,psxzr->psxyr", height_inverse, halfway, precision=lax.Precision.HIGHEST
    )
    loss_coef = loss_rate[:, None, None, None, None] * density[None, None]
    upper_settled, upper_rate = passed_along((settled[:1], loss_rate[:1]), "mom", -1)
    upper_coef = upper_rate[:, None, None, None, None] * density[None, None]
    coef_next = jnp.concatenate([loss_coef[1:], upper_coef], axis=0)
    settled_next = jnp.concatenate([settled[1:], upper_settled], axis=0)
    right_side = (1.0 - 0.5 * loss_coef) * settled + 0.5 * coef_next * settled_next
    denominator = 1.0 + 0.5 * loss_coef
    offsets = right_side / denominator
    factors = 0.5 * coef_next / denominator
    local_c = jnp.zeros(state.shape[1:], jnp.float32)
    local_g = jnp.ones(factors.shape[1:], jnp.float32)
    for level in range(bins_here - 1, -1, -1):
        local_c = offsets[level] + factors[level] * local_c
        local_g = factors[level] * local_g

    def relay_step(index, incoming):
        return passed_along(local_c + local_g * incoming, "mom", -1)

    incoming = lax.fori_loop(0, lax.axis_size("mom") - 1, relay_step, jnp.zeros_like(local_c))
    current = incoming
    levels = []
    for level in range(bins_here - 1, -1, -1):
        current = offsets[level] + factors[level] * current
        levels.append(current)
    return jnp.stack(levels[::-1], axis=0)


def local(
    spectra, production, bin_group, parent_of, diffusivity, height_inverse, loss_rate, density
):
    state = spectra
    state = one_step(
        state, production, bin_group, parent_of, diffusivity, height_inverse, loss_rate, density
    )
    return state


def solution(mesh):
    return jax.shard_map(
        local,
        mesh=mesh,
        in_specs=(
            P("mom", None, "phi", None, None),
            P(),
            P(),
            P(),
            P(),
            P(),
            P("mom"),
            P("phi", None, None),
        ),
        out_specs=P("mom", None, "phi", None, None),
        check_vma=False,
    )
```

profile of v0, /device:TPU:0, one launch (start us, length us, event | category | flops | bytes accessed | tf_op | source)
XLA Modules:
  0.0 232.6 jit_solution(12985421989858237578)
XLA Ops:
  6.5 0.0 copy-start
  6.5 0.0 all-gather.2.cloned.1.call-start
  6.5 8.7 %convert_bitcast_fusion = bf16[8,4,2,64,256]{4,1,3,2,0:T(4,128)(2,1)S(1)} fusion(f32[8,4,2,64,256]{4,3,2,1,0:T(8,128)} %param.10, s32[4]{0:T(128)} %param.13), kind=kOutput, calls=%fused_computation.29 | convolution fusion | flops 51380240 | bytes 6291472 | tf_op jit(solution)/shard_map/st,qtxzr->qsxzr/dot_general | solution.py:37
  15.3 0.4 copy.12
  15.7 0.0 copy-start.7
  15.7 0.0 copy-start.8
  15.7 0.0 copy-start.4
  15.7 2.5 %copy.16 = bf16[1,8,512,256]{3,1,2,0:T(8,128)(2,1)} copy(bf16[1,8,512,256]{3,2,1,0:T(8,128)(2,1)S(1)} %bitcast.138) | data formatting | bytes 4194304
  18.2 0.0 all-gather.2.cloned.1.call-update
  18.2 0.0 copy-done.7
  18.2 1.3 collective-permute-start.3
  19.6 0.0 copy-done.8
  19.6 0.1 dynamic-slice
  19.6 0.0 copy-done.4
  19.6 0.2 broadcast_multiply_fusion
  19.8 88.9 %all-gather.2.cloned.1.call-done = bf16[32,131072]{1,0:T(8,128)(2,1)} async-done(((bf16[8,131072]{1,0:T(8,128)(2,1)}), bf16[32,131072]{1,0:T(8,128)(2,1)}) %all-gather.2.cloned.1.call-update) | async-done | bytes 8388624 | tf_op jit(solution)/shard_map/all_gather | solution.py:47
  108.7 0.0 copy-start.3
  108.7 4.8 %fusion.29 = f32[8,131072]{1,0:T(8,128)S(1)} fusion(bf16[32,131072]{1,0:T(8,128)(2,1)} %all-gather.2.cloned.1.call-done, bf16[32,32]{1,0:T(8,128)(2,1)} %param.11, s32[]{:T(128)S(6)} %select_n.8, s32[32]{0:T(128)S(1)} %copy-done.8, s32[8]{0:T(128)S(1)} %dynamic-slice), kind=kOutput, calls=%fused_computation.76 | convolution fusion | flops 67109376 | bytes 12585124 | tf_op jit(solution)/shard_map/dot_general | solution.py:45
  113.5 0.0 copy-done.3
  113.5 1.6 fusion.42
  115.2 0.0 copy-start.5
  115.2 0.2 fusion.43
  115.4 0.2 collective-permute-start.1
  115.7 3.5 %collective-permute-start.2 = (bf16[8,4,1,64,256]{4,3,2,1,0:T(8,128)(2,1)S(1)}, bf16[8,4,1,64,256]{4,3,2,1,0:T(8,128)(2,1)S(1)}, u32[]{:S(2)}, u32[]{:S(2)}) collective-permute-start(bf16[8,4,1,64,256]{4,3,2,1,0:T(8,128)(2,1)S(1)} %get-tuple-element.43), channel_id=1, source_target_pairs={{4,0},{8,4},{12,8},{16,12},{20,16},{24,20},{28,24},{0,28},{5,1},{9... | collective-permute-start | bytes 3145736 | tf_op jit(solution)/shard_map/ppermute | solution.py:16
  119.2 0.0 copy-done.5
  119.2 0.2 fusion.44
  119.4 0.3 fusion.27
  119.7 0.0 collective-permute-done.3
  119.7 0.6 multiply_bitcast_fusion.1
  120.4 0.3 fusion.25
  120.7 20.4 %collective-permute-done.1 = bf16[8,4,1,64,256]{4,3,2,1,0:T(8,128)(2,1)S(1)} collective-permute-done((bf16[8,4,1,64,256]{4,3,2,1,0:T(8,128)(2,1)S(1)}, bf16[8,4,1,64,256]{4,3,2,1,0:T(8,128)(2,1)S(1)}, u32[]{:S(2)}, u32[]{:S(2)}) %collective-permute-start.1) | collective-permute-done | bytes 1048608 | tf_op jit(solution)/shard_map/ppermute | solution.py:14
  141.0 0.0 collective-permute-done.2
  141.0 0.6 maximum_convert_fusion
  141.7 2.9 %fusion.9 = f32[8,4,2,64,256]{4,3,2,1,0:T(8,128)S(1)} fusion(f32[8,4,2,64,256]{4,3,2,1,0:T(8,128)S(1)} %get-tuple-element.41, f32[8,4,4,64,256]{4,3,2,1,0:T(8,128)S(1)} %maximum_convert_fusion, f32[64,256]{1,0:T(8,128)S(1)} %broadcast_multiply_fusion.2, f32[64,256]{1,0:T(8,128)S(1)} %copy-done.5), kind=kLoop, calls=%fused_computation.13 | loop fusion | flops 9437184 | bytes 16908288 | tf_op jit(solution)/shard_map/add | solution.py:55
  144.5 0.0 copy-done
  144.6 5.4 %fusion.18 = f32[8,4,2,64,256]{4,3,2,1,0:T(8,128)S(1)} fusion(f32[8,4,2,64,256]{4,3,2,1,0:T(8,128)S(1)} %fusion.9, f32[64,64]{1,0:T(8,128)S(1)} %copy-done), kind=kOutput, calls=%fused_computation.26 | convolution fusion | flops 810549248 | bytes 8404992 | tf_op jit(solution)/shard_map/yz,psxzr->psxyr/dot_general | solution.py:58
  150.0 1.3 collective-permute-start.4
  151.3 0.1 maximum_multiply_fusion.1
  151.4 0.1 slice_bitcast_fusion.8
  151.5 0.4 slice.141
  152.0 14.0 %collective-permute-done.4 = f32[1,4,2,64,256]{4,3,2,1,0:T(8,128)S(1)} collective-permute-done((f32[1,4,2,64,256]{4,3,2,1,0:T(8,128)S(1)}, f32[1,4,2,64,256]{4,3,2,1,0:T(8,128)S(1)}, u32[]{:S(2)}, u32[]{:S(2)}) %collective-permute-start.4) | collective-permute-done | bytes 524320 | tf_op jit(solution)/shard_map/ppermute | solution.py:26
  166.0 1.6 fusion.14
  167.6 0.0 copy-start.1
  167.7 2.0 copy-done.1
  169.7 0.4 multiply_add_fusion.8
  170.1 48.9 %while.10 = (s32[]{:T(128)}, f32[4,2,64,256]{3,2,1,0:T(8,128)S(1)}, f32[1,2,64,256]{3,2,1,0:T(8,128)S(1)}, f32[4,2,64,256]{3,2,1,0:T(8,128)S(1)}, s32[]{:T(128)}) while((s32[]{:T(128)}, f32[4,2,64,256]{3,2,1,0:T(8,128)S(1)}, f32[1,2,64,256]{3,2,1,0:T(8,128)S(1)}, f32[4,2,64,256]{3,2,1,0:T(8,128)S(1)}, s32[]{:T(128)}) %tuple.34), condition=%wide.region_1.2_spmd, body=%wide.region_0.1_spmd.sunk | while | flops 262146 | bytes 3801189 | solution.py:79
  170.1 0.1 multiply_add_fusion.13
  170.2 1.3 collective-permute-start
  171.5 15.6 %collective-permute-done = f32[4,2,64,256]{3,2,1,0:T(8,128)S(1)} collective-permute-done((f32[4,2,64,256]{3,2,1,0:T(8,128)S(1)}, f32[4,2,64,256]{3,2,1,0:T(8,128)S(1)}, u32[]{:S(2)}, u32[]{:S(2)}) %collective-permute-start) | collective-permute-done | bytes 524320 | tf_op jit(solution)/shard_map/while/body/eval_jaxpr/ppermute | solution.py:26
  187.1 0.1 multiply_add_fusion.13
  187.2 1.3 collective-permute-start
  188.5 15.0 %collective-permute-done = f32[4,2,64,256]{3,2,1,0:T(8,128)S(1)} collective-permute-done((f32[4,2,64,256]{3,2,1,0:T(8,128)S(1)}, f32[4,2,64,256]{3,2,1,0:T(8,128)S(1)}, u32[]{:S(2)}, u32[]{:S(2)}) %collective-permute-start) | collective-permute-done | bytes 524320 | tf_op jit(solution)/shard_map/while/body/eval_jaxpr/ppermute | solution.py:26
  203.5 0.1 multiply_add_fusion.13
  203.6 1.3 collective-permute-start
  204.9 14.1 %collective-permute-done = f32[4,2,64,256]{3,2,1,0:T(8,128)S(1)} collective-permute-done((f32[4,2,64,256]{3,2,1,0:T(8,128)S(1)}, f32[4,2,64,256]{3,2,1,0:T(8,128)S(1)}, u32[]{:S(2)}, u32[]{:S(2)}) %collective-permute-start) | collective-permute-done | bytes 524320 | tf_op jit(solution)/shard_map/while/body/eval_jaxpr/ppermute | solution.py:26
  219.0 0.0 copy-start.2
  219.0 2.8 %bitcast_dynamic-update-slice_fusion.7 = (f32[8,4,2,64,256]{4,3,2,1,0:T(8,128)S(1)}, f32[4,2,64,256]{3,2,1,0:T(8,128)S(1)}, f32[4,2,64,256]{3,2,1,0:T(8,128)S(1)}, f32[4,2,64,256]{3,2,1,0:T(8,128)S(1)}) fusion(f32[8,4,2,64,256]{4,3,2,1,0:T(8,128)} %copy-done.1, f32[2,64,256]{2,1,0:T(8,128)S(1)} %get-tuple-element.52, ...), kind=kLoop, calls=%fused_computation.51 | loop fusion | flops 2097151 | bytes 7864320
  221.8 0.7 copy-done.2
  222.5 0.1 bitcast_dynamic-update-slice_fusion.6
  222.6 0.1 bitcast_dynamic-update-slice_fusion.4
  222.7 0.1 bitcast_dynamic-update-slice_fusion.2
  222.9 0.0 copy-start.6
  222.9 2.0 copy-done.6
  224.9 0.9 bitcast_dynamic-update-slice_fusion
  (7 shorter events, 0.2 us)
Async XLA Ops:
  6.5 138.0 %copy-start = (f32[64,64]{1,0:T(8,128)S(1)}, f32[64,64]{1,0:T(8,128)}, u32[]{:S(2)}) copy-start(f32[64,64]{1,0:T(8,128)} %param.15) | copy-start | bytes 49156
  6.5 102.2 %all-gather.2.cloned.1.call-start = ((), (), s32[]{:S(2)}) async-start(), calls=%async_computation | async-start | bytes 10485760 | tf_op jit(solution)/shard_map/all_gather | solution.py:47
  15.7 2.6 %copy-start.7 = (f32[8]{0:T(128)S(1)}, f32[8]{0:T(128)}, u32[]{:S(2)}) copy-start(f32[8]{0:T(128)} %param.16) | copy-start | bytes 100
  15.7 3.9 %copy-start.8 = (s32[32]{0:T(128)S(1)}, s32[32]{0:T(128)}, u32[]{:S(2)}) copy-start(s32[32]{0:T(128)} %param.12) | copy-start | bytes 388
  15.7 4.0 %copy-start.4 = (f32[2,64,256]{2,1,0:T(8,128)S(1)}, f32[2,64,256]{2,1,0:T(8,128)}, u32[]{:S(2)}) copy-start(f32[2,64,256]{2,1,0:T(8,128)} %param.17) | copy-start | bytes 393220
  18.2 101.5 %collective-permute-start.3 = (f32[1]{0:T(128)S(1)}, f32[1]{0:T(128)}, u32[]{:S(2)}, u32[]{:S(2)}) collective-permute-start(f32[1]{0:T(128)S(1)} %bitcast.140), channel_id=1, source_target_pairs={{1,0},{2,1},{3,2},{5,4},{6,5},{7,6},{9,8},{10,9},{11,10},{13,12},{... | collective-permute-start | bytes 20 | tf_op jit(solution)/shard_map/ppermute | solution.py:26
  108.7 4.8 %copy-start.3 = (f32[8,4,2,64,256]{4,3,2,1,0:T(8,128)S(1)}, f32[8,4,2,64,256]{4,3,2,1,0:T(8,128)}, u32[]{:S(2)}) copy-start(f32[8,4,2,64,256]{4,3,2,1,0:T(8,128)} %param.10) | copy-start | bytes 12582916
  115.2 4.0 %copy-start.5 = (f32[64,256]{1,0:T(8,128)S(1)}, f32[64,256]{1,0:T(8,128)}, u32[]{:S(2)}) copy-start(f32[64,256]{1,0:T(8,128)} %param.14) | copy-start | bytes 196612
  115.4 25.6 %collective-permute-start.1 = (bf16[8,4,1,64,256]{4,3,2,1,0:T(8,128)(2,1)S(1)}, bf16[8,4,1,64,256]{4,3,2,1,0:T(8,128)(2,1)S(1)}, u32[]{:S(2)}, u32[]{:S(2)}) collective-permute-start(bf16[8,4,1,64,256]{4,3,2,1,0:T(8,128)(2,1)S(1)} %get-tuple-element.42), channel_id=1, source_target_pairs={{0,4},{4,8},{8,12},{12,16},{16,20},{20,24},{24,28},{28,0},{1,5},{5... | collective-permute-start | bytes 3145736 | tf_op jit(solution)/shard_map/ppermute | solution.py:14
  115.7 25.4 %collective-permute-start.2 = (bf16[8,4,1,64,256]{4,3,2,1,0:T(8,128)(2,1)S(1)}, bf16[8,4,1,64,256]{4,3,2,1,0:T(8,128)(2,1)S(1)}, u32[]{:S(2)}, u32[]{:S(2)}) collective-permute-start(bf16[8,4,1,64,256]{4,3,2,1,0:T(8,128)(2,1)S(1)} %get-tuple-element.43), channel_id=1, source_target_pairs={{4,0},{8,4},{12,8},{16,12},{20,16},{24,20},{28,24},{0,28},{5,1},{9... | collective-permute-start | bytes 3145736 | tf_op jit(solution)/shard_map/ppermute | solution.py:16
  150.0 16.0 %collective-permute-start.4 = (f32[1,4,2,64,256]{4,3,2,1,0:T(8,128)S(1)}, f32[1,4,2,64,256]{4,3,2,1,0:T(8,128)S(1)}, u32[]{:S(2)}, u32[]{:S(2)}) collective-permute-start(f32[1,4,2,64,256]{4,3,2,1,0:T(8,128)S(1)} %slice.142), channel_id=1, source_target_pairs={{1,0},{2,1},{3,2},{5,4},{6,5},{7,6},{9,8},{10,9},{11,10},{13,12},{... | collective-permute-start | bytes 1572872 | tf_op jit(solution)/shard_map/ppermute | solution.py:26
  167.6 2.0 copy-start.1
  170.2 16.9 %collective-permute-start = (f32[4,2,64,256]{3,2,1,0:T(8,128)S(1)}, f32[4,2,64,256]{3,2,1,0:T(8,128)S(1)}, u32[]{:S(2)}, u32[]{:S(2)}) collective-permute-start(f32[4,2,64,256]{3,2,1,0:T(8,128)S(1)} %multiply_add_fusion.13), channel_id=1, source_target_pairs={{1,0},{2,1},{3,2},{5,4},{6,5},{7,6},{9,8},{10,9},{11,10},{13,12},{... | collective-permute-start | bytes 1572872 | tf_op jit(solution)/shard_map/while/body/eval_jaxpr/ppermute | solution.py:26
  187.2 16.3 %collective-permute-start = (f32[4,2,64,256]{3,2,1,0:T(8,128)S(1)}, f32[4,2,64,256]{3,2,1,0:T(8,128)S(1)}, u32[]{:S(2)}, u32[]{:S(2)}) collective-permute-start(f32[4,2,64,256]{3,2,1,0:T(8,128)S(1)} %multiply_add_fusion.13), channel_id=1, source_target_pairs={{1,0},{2,1},{3,2},{5,4},{6,5},{7,6},{9,8},{10,9},{11,10},{13,12},{... | collective-permute-start | bytes 1572872 | tf_op jit(solution)/shard_map/while/body/eval_jaxpr/ppermute | solution.py:26
  203.6 15.4 %collective-permute-start = (f32[4,2,64,256]{3,2,1,0:T(8,128)S(1)}, f32[4,2,64,256]{3,2,1,0:T(8,128)S(1)}, u32[]{:S(2)}, u32[]{:S(2)}) collective-permute-start(f32[4,2,64,256]{3,2,1,0:T(8,128)S(1)} %multiply_add_fusion.13), channel_id=1, source_target_pairs={{1,0},{2,1},{3,2},{5,4},{6,5},{7,6},{9,8},{10,9},{11,10},{13,12},{... | collective-permute-start | bytes 1572872 | tf_op jit(solution)/shard_map/while/body/eval_jaxpr/ppermute | solution.py:26
  219.0 3.4 %copy-start.2 = (f32[8,4,2,64,256]{4,3,2,1,0:T(8,128)S(1)}, f32[8,4,2,64,256]{4,3,2,1,0:T(8,128)}, u32[]{:S(2)}) copy-start(f32[8,4,2,64,256]{4,3,2,1,0:T(8,128)} %copy-done.1) | copy-start | bytes 12582916
  222.9 2.0 copy-start.6
Sparse Core Ops, SparseCore 0:
  18.4 90.2 all-gather.1
where the time goes:
time: 233 us
  waiting for transfers between devices  168 us (72%)
  matrix products  18.9 us (8%)
  between operations  13.7 us (6%)
  other arithmetic  12.9 us (6%)
  starting transfers between devices  10.2 us (4%)
  local copies, waits for them, and re-layouts  8.76 us (4%)
    all_gather x1, waiting for transfers between devices, one_step(): lax.all_gather(flat_parents, 'mom', axis=0, tiled=True)  88.9 us
    ppermute x5, waiting for transfers between devices, passed_along(): return lax.ppermute(block, axis, route)  58.8 us
    ppermute x1, waiting for transfers between devices, padded_2(): lax.ppermute(tail, axis, [(i, (i + 1) % count) for i in range(count)])  20.4 us
    dot_general x1, matrix products, one_step(): jnp.einsum('st,qtxzr->qsxzr', onehot, state, precision=lax.Precision.HIGH...  8.71 us
    unnamed x22, local copies, waits for them, and re-layouts  7.36 us
    ppermute x5, starting transfers between devices, passed_along(): return lax.ppermute(block, axis, route)  6.46 us
    dot_general x1, matrix products, one_step(): jnp.einsum('yz,psxzr->psxyr', height_inverse, halfway, precision=lax.Prec...  5.41 us
    dot_general x1, matrix products, one_step(): jnp.dot(kernel_rows, lax.all_gather(flat_parents, 'mom', axis=0, tiled=Tr...  4.81 us
  transfers between devices with their start and end apart: 8, of which 6 were waited for; matrix products, arithmetic and copies ran while one was open for 4% of the time, Pallas kernels for 0%

commit v1 on v0

--- a/solution.py
+++ b/solution.py
@@ -1,7 +1,41 @@
+import functools
 import jax
 import jax.numpy as jnp
 from jax import lax
 from jax.sharding import PartitionSpec as P
+
+
+def report_bands_for(frame, array_dim):
+    frame = jnp.moveaxis(frame, 0, array_dim)
+    next_value = frame.shape
+    return frame.reshape(
+        *next_value[:array_dim],
+        next_value[array_dim] * next_value[array_dim + 1],
+        *next_value[array_dim + 2 :]
+    )
+
+
+def _direct_bars(view, dev_axis, ndim_at):
+    n = lax.axis_size(dev_axis)
+    panels = [(i0, (i0 + 1) % n) for i0 in range(n)]
+    kept_rows = [(j0, p) for p, j0 in panels]
+    new, v_now = ([], [])
+    for no in tuple(range(n - 1)):
+        if no % 2 == 0:
+            block_last = lax.ppermute(new[-1] if new else view, dev_axis, panels)
+            new.append(block_last)
+        else:
+            taken_in = lax.ppermute(v_now[-1] if v_now else view, dev_axis, kept_rows)
+            v_now.append(taken_in)
+    r_now = jnp.stack([*new[::-1], view, *v_now])
+    upper = len(new)
+    block_out = lax.axis_index(dev_axis)
+    carry_in = block_out - upper
+    r_now = r_now[(jnp.arange(n) - carry_in) % n]
+    return report_bands_for(r_now, ndim_at)
+
+
+register_chains = functools.partial(_direct_bars, dev_axis="mom", ndim_at=0)
 
 
 def padded_2(cells, sides, width):
@@ -42,11 +76,7 @@
     first_bin = lax.axis_index("mom") * bins_here
     flat_parents = parents.reshape(bins_here, -1)
     kernel_rows = lax.dynamic_slice_in_dim(kernel, first_bin, bins_here, 0)
-    source = jnp.dot(
-        kernel_rows,
-        lax.all_gather(flat_parents, "mom", axis=0, tiled=True),
-        preferred_element_type=jnp.float32,
-    )
+    source = jnp.dot(kernel_rows, register_chains(flat_parents), preferred_element_type=jnp.float32)
     sourced = state + source.reshape(state.shape)
     padded = padded_2(sourced.astype(jnp.bfloat16), (("phi", 2),), 1).astype(sourced.dtype)
     lap_phi = padded[:, :, 2:] + padded[:, :, :-2] - 2.0 * sourced

time: 233 us -> 306 us (1.31)
  waiting for transfers between devices: 168 us -> 209 us
  local copies, waits for them, and re-layouts: 8.76 us -> 33.3 us
  between operations: 13.7 us -> 0.33 us
  other arithmetic: 12.9 us -> 23.6 us
  matrix products: 18.9 us -> 24.1 us
  starting transfers between devices: 10.2 us -> 15.2 us
    ppermute x0 -> x3, waiting for transfers between devices: none -> 131 us  [the longest x2 90.3 us: _direct_bars(): block_last = lax.ppermute(new[-1] if new else view, dev_axis, panels)]
    all_gather x1 -> x0, waiting for transfers between devices: 88.9 us -> none  [one_step(): lax.all_gather(flat_parents, 'mom', axis=0, tiled=True)]
    gather x0 -> x3, local copies, waits for them, and re-layouts: none -> 13.6 us  [_direct_bars(): r_now = r_now[(jnp.arange(n) - carry_in) % n]]
    unnamed x22 -> x23, local copies, waits for them, and re-layouts: 7.36 us -> 16.1 us
    unnamed x4 -> x5, other arithmetic: 2.99 us -> 10.3 us
    ppermute x0 -> x3, starting transfers between devices: none -> 5 us  [the longest x2 4.04 us: _direct_bars(): block_last = lax.ppermute(new[-1] if new else view, dev_axis, panels)]
    dot_general x1, matrix products: 4.81 us -> 9.77 us  [one_step(): jnp.dot(kernel_rows, register_chains(flat_parents), preferred_element_typ...]
    another operation x0 -> x1, other arithmetic: none -> 4.34 us  [_direct_bars(): r_now = jnp.stack([*new[::-1], view, *v_now])]
  transfers between devices with their start and end apart: 8 -> 10, of which waited for: 6 -> 8; matrix products, arithmetic and copies ran while one was open for 4% -> 16% of each run, Pallas kernels for 0% -> 0%
where the time goes in v1:
time: 306 us
  waiting for transfers between devices  209 us (68%)
  local copies, waits for them, and re-layouts  33.3 us (11%)
  matrix products  24.1 us (8%)
  other arithmetic  23.6 us (8%)
  starting transfers between devices  15.2 us (5%)
    ppermute x2, waiting for transfers between devices, _direct_bars(): block_last = lax.ppermute(new[-1] if new else view, dev_axis, panels)  90.3 us
    ppermute x5, waiting for transfers between devices, passed_along(): return lax.ppermute(block, axis, route)  58.9 us
    ppermute x1, waiting for transfers between devices, _direct_bars(): taken_in = lax.ppermute(v_now[-1] if v_now else view, dev_axis, kept_rows)  40.3 us
    ppermute x1, waiting for transfers between devices, padded_2(): lax.ppermute(tail, axis, [(i, (i + 1) % count) for i in range(count)])  19.9 us
    unnamed x23, local copies, waits for them, and re-layouts  16.1 us
    gather x3, local copies, waits for them, and re-layouts, _direct_bars(): r_now = r_now[(jnp.arange(n) - carry_in) % n]  13.6 us
    unnamed x5, other arithmetic  10.3 us
    dot_general x1, matrix products, one_step(): jnp.dot(kernel_rows, register_chains(flat_parents), preferred_element_typ...  9.77 us
  transfers between devices with their start and end apart: 10, of which 8 were waited for; matrix products, arithmetic and copies ran while one was open for 16% of the time, Pallas kernels for 0%

profile of v1, /device:TPU:0, one launch (start us, length us, event | category | flops | bytes accessed | tf_op | source)
XLA Modules:
  0.0 305.9 jit_solution(7864482328595004846)
XLA Ops:
  0.0 8.7 %convert_bitcast_fusion = bf16[8,4,2,64,256]{4,1,3,2,0:T(4,128)(2,1)S(1)} fusion(f32[8,4,2,64,256]{4,3,2,1,0:T(8,128)} %param.10, s32[4]{0:T(128)} %param.13), kind=kOutput, calls=%fused_computation.28 | convolution fusion | flops 51380240 | bytes 6291472 | tf_op jit(solution)/shard_map/st,qtxzr->qsxzr/dot_general | solution.py:71
  8.7 0.0 copy-start.7
  8.7 0.4 copy.13
  9.1 0.0 copy-start.8
  9.1 0.0 copy-start.4
  9.2 2.5 copy.21
  11.7 2.9 collective-permute-start.1
  14.6 1.0 collective-permute-start.3
  15.6 46.8 %collective-permute-done.1 = bf16[8,131072]{1,0:T(8,128)(2,1)} collective-permute-done((bf16[8,131072]{1,0:T(8,128)(2,1)}, bf16[8,131072]{1,0:T(8,128)(2,1)}, u32[]{:S(2)}, u32[]{:S(2)}) %collective-permute-start.1) | collective-permute-done | bytes 2097184 | tf_op jit(solution)/shard_map/ppermute | solution.py:25
  62.3 1.1 collective-permute-start.2
  63.4 1.5 collective-permute-start.6
  64.9 2.3 stack_reshape.3
  67.2 0.1 dynamic-slice
  67.3 0.2 broadcast_multiply_fusion
  67.5 40.3 %collective-permute-done.3 = bf16[8,131072]{1,0:T(8,128)(2,1)} collective-permute-done((bf16[8,131072]{1,0:T(8,128)(2,1)}, bf16[8,131072]{1,0:T(8,128)(2,1)}, u32[]{:S(2)}, u32[]{:S(2)}) %collective-permute-start.3) | collective-permute-done | bytes 2097184 | tf_op jit(solution)/shard_map/ppermute | solution.py:28
  107.8 43.5 %collective-permute-done.2 = bf16[8,131072]{1,0:T(8,128)(2,1)} collective-permute-done((bf16[8,131072]{1,0:T(8,128)(2,1)}, bf16[8,131072]{1,0:T(8,128)(2,1)}, u32[]{:S(2)}, u32[]{:S(2)}) %collective-permute-start.2) | collective-permute-done | bytes 2097184 | tf_op jit(solution)/shard_map/ppermute | solution.py:25
  151.4 4.3 %pad_maximum_fusion = bf16[4,8,131072]{2,1,0:T(8,128)(2,1)S(1)} fusion(bf16[1,8,131072]{2,1,0:T(8,128)(2,1)} %bitcast.8, bf16[1,8,131072]{2,1,0:T(8,128)(2,1)} %stack_reshape.3, bf16[1,8,131072]{2,1,0:T(8,128)(2,1)} %bitcast.7, bf16[1,8,131072]{2,1,0:T(8,128)(2,1)} %bitcast.6), kind=kLoop, calls=%fused_computation.3 | loop fusion | flops 12582912 | bytes 16777216 | tf_op jit(solution)/shard_map/stack | solution.py:30
  155.7 3.6 %fusion.39 = (bf16[4,8,65536]{2,1,0:T(8,128)(2,1)}, bf16[4,8,65536]{2,1,0:T(8,128)(2,1)}) fusion(bf16[4,8,131072]{2,1,0:T(8,128)(2,1)S(1)} %pad_maximum_fusion), kind=kLoop, calls=%fused_computation.93 | loop fusion | bytes 16777216 | tf_op jit(solution)/shard_map/gather | solution.py:34
  159.3 5.0 %gather_fusion = bf16[4,8,65536]{2,1,0:T(8,128)(2,1)} fusion(bf16[4,8,65536]{2,1,0:T(8,128)(2,1)} %get-tuple-element.40, s32[1024]{0:T(1024)S(1)} %pad_clamp_fusion), kind=kCustom, calls=%fused_computation | custom fusion | bytes 8388624 | tf_op jit(solution)/shard_map/gather | solution.py:34
  164.3 5.0 %gather_fusion.1 = bf16[4,8,65536]{2,1,0:T(8,128)(2,1)} fusion(bf16[4,8,65536]{2,1,0:T(8,128)(2,1)} %get-tuple-element.41, s32[1024]{0:T(1024)S(1)} %pad_clamp_fusion), kind=kCustom, calls=%fused_computation.1 | custom fusion | bytes 8388624 | tf_op jit(solution)/shard_map/gather | solution.py:34
  169.3 7.3 %pad_maximum_fusion.1 = bf16[4,8,131072]{2,1,0:T(8,128)(2,1)} fusion(bf16[4,8,65536]{2,1,0:T(8,128)(2,1)} %gather_fusion.1, bf16[4,8,65536]{2,1,0:T(8,128)(2,1)} %gather_fusion), kind=kLoop, calls=%fused_computation.4 | loop fusion | flops 16777216 | bytes 16777216
  176.6 8.8 %copy.22 = bf16[4,8,512,256]{3,2,1,0:T(8,128)(2,1)} copy(bf16[4,8,512,256]{3,1,2,0:T(8,128)(2,1)} %bitcast.157) | data formatting | bytes 16777216
  185.4 9.8 %fusion.42 = (bf16[8,4,2,64,256]{4,0,3,2,1:T(8,128)(2,1)S(1)}, f32[8,4,2,64,256]{4,0,3,2,1:T(8,128)S(1)}) fusion(bf16[4,2,64,256,32]{3,2,1,0,4:T(8,128)(2,1)} %bitcast.156, bf16[32,32]{1,0:T(8,128)(2,1)} %param.11, s32[]{:T(128)S(6)} %select_n.32, s32[32]{0:T(128)S(1)} %copy-done.8, s32[8]{0:T(128)S(1)} %dynamic-slice, f32[8,4,2,64,256]{4,3,2,1,0:T(8,128)S(1)} %copy-done.3), kind=kOutput, calls=%fused_computation.96 | convolution fusion | flops 69206528 | bytes 18876580 | tf_op jit(solution)/shard_map/dot_general | solution.py:79
  195.2 0.0 copy-start.5
  195.2 0.1 fusion.40
  195.3 0.1 collective-permute-start.4
  195.4 3.5 %collective-permute-start.5 = (bf16[8,4,1,64,256]{4,0,3,2,1:T(8,128)(2,1)S(1)}, bf16[8,4,1,64,256]{4,0,3,2,1:T(8,128)(2,1)S(1)}, u32[]{:S(2)}, u32[]{:S(2)}) collective-permute-start(bf16[8,4,1,64,256]{4,0,3,2,1:T(8,128)(2,1)S(1)} %get-tuple-element.43), channel_id=1, source_target_pairs={{4,0},{8,4},{12,8},{16,12},{20,16},{24,20},{28,24},{0,28},{5,1},{9... | collective-permute-start | bytes 3145736 | tf_op jit(solution)/shard_map/ppermute | solution.py:50
  198.9 0.1 fusion.41
  199.1 0.3 fusion.24
  199.4 0.0 collective-permute-done.6
  199.4 0.7 multiply_bitcast_fusion.1
  200.1 0.3 fusion.22
  200.4 19.9 %collective-permute-done.4 = bf16[8,4,1,64,256]{4,0,3,2,1:T(8,128)(2,1)S(1)} collective-permute-done((bf16[8,4,1,64,256]{4,0,3,2,1:T(8,128)(2,1)S(1)}, bf16[8,4,1,64,256]{4,0,3,2,1:T(8,128)(2,1)S(1)}, u32[]{:S(2)}, u32[]{:S(2)}) %collective-permute-start.4) | collective-permute-done | bytes 1048608 | tf_op jit(solution)/shard_map/ppermute | solution.py:48
  220.3 0.7 maximum_convert_fusion
  220.9 2.7 fusion.5
  223.6 0.7 multiply_add_fusion.1
  224.3 5.6 %fusion.15 = f32[8,4,2,64,256]{4,3,2,1,0:T(8,128)S(1)} fusion(f32[8,4,2,64,256]{4,0,3,2,1:T(8,128)S(1)} %multiply_add_fusion.1, f32[64,64]{1,0:T(8,128)S(1)} %copy-done), kind=kOutput, calls=%fused_computation.27 | convolution fusion | flops 805306368 | bytes 8404992 | tf_op jit(solution)/shard_map/yz,psxzr->psxyr/dot_general | solution.py:88
  230.0 1.3 collective-permute-start.7
  231.3 0.1 maximum_multiply_fusion.1
  231.4 0.1 slice_bitcast_fusion.8
  231.5 0.4 slice.145
  231.9 13.5 %collective-permute-done.7 = f32[1,4,2,64,256]{4,3,2,1,0:T(8,128)S(1)} collective-permute-done((f32[1,4,2,64,256]{4,3,2,1,0:T(8,128)S(1)}, f32[1,4,2,64,256]{4,3,2,1,0:T(8,128)S(1)}, u32[]{:S(2)}, u32[]{:S(2)}) %collective-permute-start.7) | collective-permute-done | bytes 524320 | tf_op jit(solution)/shard_map/ppermute | solution.py:60
  245.4 1.7 fusion.10
  247.2 0.0 copy-start.1
  247.2 2.0 copy-done.1
  249.2 0.4 multiply_add_fusion.9
  249.6 49.5 %while.10 = (s32[]{:T(128)}, f32[4,2,64,256]{3,2,1,0:T(8,128)S(1)}, f32[1,2,64,256]{3,2,1,0:T(8,128)S(1)}, f32[4,2,64,256]{3,2,1,0:T(8,128)S(1)}, s32[]{:T(128)}) while((s32[]{:T(128)}, f32[4,2,64,256]{3,2,1,0:T(8,128)S(1)}, f32[1,2,64,256]{3,2,1,0:T(8,128)S(1)}, f32[4,2,64,256]{3,2,1,0:T(8,128)S(1)}, s32[]{:T(128)}) %tuple.35), condition=%wide.region_1.2_spmd, body=%wide.region_0.1_spmd.sunk | while | flops 262146 | bytes 3801189 | solution.py:109
  249.7 0.1 multiply_add_fusion.14
  249.7 1.3 collective-permute-start
  251.0 15.3 %collective-permute-done = f32[4,2,64,256]{3,2,1,0:T(8,128)S(1)} collective-permute-done((f32[4,2,64,256]{3,2,1,0:T(8,128)S(1)}, f32[4,2,64,256]{3,2,1,0:T(8,128)S(1)}, u32[]{:S(2)}, u32[]{:S(2)}) %collective-permute-start) | collective-permute-done | bytes 524320 | tf_op jit(solution)/shard_map/while/body/eval_jaxpr/ppermute | solution.py:60
  266.4 0.1 multiply_add_fusion.14
  266.5 1.3 collective-permute-start
  267.8 15.6 %collective-permute-done = f32[4,2,64,256]{3,2,1,0:T(8,128)S(1)} collective-permute-done((f32[4,2,64,256]{3,2,1,0:T(8,128)S(1)}, f32[4,2,64,256]{3,2,1,0:T(8,128)S(1)}, u32[]{:S(2)}, u32[]{:S(2)}) %collective-permute-start) | collective-permute-done | bytes 524320 | tf_op jit(solution)/shard_map/while/body/eval_jaxpr/ppermute | solution.py:60
  283.4 0.1 multiply_add_fusion.14
  283.4 1.3 collective-permute-start
  284.7 14.4 %collective-permute-done = f32[4,2,64,256]{3,2,1,0:T(8,128)S(1)} collective-permute-done((f32[4,2,64,256]{3,2,1,0:T(8,128)S(1)}, f32[4,2,64,256]{3,2,1,0:T(8,128)S(1)}, u32[]{:S(2)}, u32[]{:S(2)}) %collective-permute-start) | collective-permute-done | bytes 524320 | tf_op jit(solution)/shard_map/while/body/eval_jaxpr/ppermute | solution.py:60
  299.2 2.8 bitcast_dynamic-update-slice_fusion.7
  302.0 0.7 copy-done.2
  302.6 0.1 bitcast_dynamic-update-slice_fusion.6
  302.8 0.1 bitcast_dynamic-update-slice_fusion.4
  302.9 0.1 bitcast_dynamic-update-slice_fusion.2
  303.0 0.0 copy-start.6
  303.0 2.0 copy-done.6
  305.1 0.9 bitcast_dynamic-update-slice_fusion
  (19 shorter events, 0.2 us)
Async XLA Ops:
  0.0 224.3 %copy-start = (f32[64,64]{1,0:T(8,128)S(1)}, f32[64,64]{1,0:T(8,128)}, u32[]{:S(2)}) copy-start(f32[64,64]{1,0:T(8,128)} %param.15) | copy-start | bytes 49156
  8.7 54.7 %copy-start.7 = (f32[8]{0:T(128)S(1)}, f32[8]{0:T(128)}, u32[]{:S(2)}) copy-start(f32[8]{0:T(128)} %param.16) | copy-start | bytes 100
  9.1 58.1 %copy-start.8 = (s32[32]{0:T(128)S(1)}, s32[32]{0:T(128)}, u32[]{:S(2)}) copy-start(s32[32]{0:T(128)} %param.12) | copy-start | bytes 388
  9.1 58.2 %copy-start.4 = (f32[2,64,256]{2,1,0:T(8,128)S(1)}, f32[2,64,256]{2,1,0:T(8,128)}, u32[]{:S(2)}) copy-start(f32[2,64,256]{2,1,0:T(8,128)} %param.17) | copy-start | bytes 393220
  11.7 50.7 %collective-permute-start.1 = (bf16[8,131072]{1,0:T(8,128)(2,1)}, bf16[8,131072]{1,0:T(8,128)(2,1)}, u32[]{:S(2)}, u32[]{:S(2)}) collective-permute-start(bf16[8,131072]{1,0:T(8,128)(2,1)} %bitcast.50), channel_id=1, source_target_pairs={{0,1},{1,2},{2,3},{3,0},{4,5},{5,6},{6,7},{7,4},{8,9},{9,10},{10,1... | collective-permute-start | bytes 6291464 | tf_op jit(solution)/shard_map/ppermute | solution.py:25
  14.6 93.2 %collective-permute-start.3 = (bf16[8,131072]{1,0:T(8,128)(2,1)}, bf16[8,131072]{1,0:T(8,128)(2,1)}, u32[]{:S(2)}, u32[]{:S(2)}) collective-permute-start(bf16[8,131072]{1,0:T(8,128)(2,1)} %bitcast.50), channel_id=1, source_target_pairs={{1,0},{2,1},{3,2},{0,3},{5,4},{6,5},{7,6},{4,7},{9,8},{10,9},{11,1... | collective-permute-start | bytes 6291464 | tf_op jit(solution)/shard_map/ppermute | solution.py:28
  62.3 89.1 %collective-permute-start.2 = (bf16[8,131072]{1,0:T(8,128)(2,1)}, bf16[8,131072]{1,0:T(8,128)(2,1)}, u32[]{:S(2)}, u32[]{:S(2)}) collective-permute-start(bf16[8,131072]{1,0:T(8,128)(2,1)} %collective-permute-done.1), channel_id=1, source_target_pairs={{0,1},{1,2},{2,3},{3,0},{4,5},{5,6},{6,7},{7,4},{8,9},{9,10},{10,1... | collective-permute-start | bytes 6291464 | tf_op jit(solution)/shard_map/ppermute | solution.py:25
  63.4 135.9 %collective-permute-start.6 = (f32[1]{0:T(128)S(1)}, f32[1]{0:T(128)}, u32[]{:S(2)}, u32[]{:S(2)}) collective-permute-start(f32[1]{0:T(128)S(1)} %bitcast.160), channel_id=1, source_target_pairs={{1,0},{2,1},{3,2},{5,4},{6,5},{7,6},{9,8},{10,9},{11,10},{13,12},{... | collective-permute-start | bytes 20 | tf_op jit(solution)/shard_map/ppermute | solution.py:60
  176.6 8.8 %copy-start.3 = (f32[8,4,2,64,256]{4,3,2,1,0:T(8,128)S(1)}, f32[8,4,2,64,256]{4,3,2,1,0:T(8,128)}, u32[]{:S(2)}) copy-start(f32[8,4,2,64,256]{4,3,2,1,0:T(8,128)} %param.10) | copy-start | bytes 12582916
  195.2 3.8 %copy-start.5 = (f32[64,256]{1,0:T(8,128)S(1)}, f32[64,256]{1,0:T(8,128)}, u32[]{:S(2)}) copy-start(f32[64,256]{1,0:T(8,128)} %param.14) | copy-start | bytes 196612
  195.3 24.9 %collective-permute-start.4 = (bf16[8,4,1,64,256]{4,0,3,2,1:T(8,128)(2,1)S(1)}, bf16[8,4,1,64,256]{4,0,3,2,1:T(8,128)(2,1)S(1)}, u32[]{:S(2)}, u32[]{:S(2)}) collective-permute-start(bf16[8,4,1,64,256]{4,0,3,2,1:T(8,128)(2,1)S(1)} %get-tuple-element.42), channel_id=1, source_target_pairs={{0,4},{4,8},{8,12},{12,16},{16,20},{20,24},{24,28},{28,0},{1,5},{5... | collective-permute-start | bytes 3145736 | tf_op jit(solution)/shard_map/ppermute | solution.py:48
  195.4 24.9 %collective-permute-start.5 = (bf16[8,4,1,64,256]{4,0,3,2,1:T(8,128)(2,1)S(1)}, bf16[8,4,1,64,256]{4,0,3,2,1:T(8,128)(2,1)S(1)}, u32[]{:S(2)}, u32[]{:S(2)}) collective-permute-start(bf16[8,4,1,64,256]{4,0,3,2,1:T(8,128)(2,1)S(1)} %get-tuple-element.43), channel_id=1, source_target_pairs={{4,0},{8,4},{12,8},{16,12},{20,16},{24,20},{28,24},{0,28},{5,1},{9... | collective-permute-start | bytes 3145736 | tf_op jit(solution)/shard_map/ppermute | solution.py:50
  230.0 15.4 %collective-permute-start.7 = (f32[1,4,2,64,256]{4,3,2,1,0:T(8,128)S(1)}, f32[1,4,2,64,256]{4,3,2,1,0:T(8,128)S(1)}, u32[]{:S(2)}, u32[]{:S(2)}) collective-permute-start(f32[1,4,2,64,256]{4,3,2,1,0:T(8,128)S(1)} %slice.146), channel_id=1, source_target_pairs={{1,0},{2,1},{3,2},{5,4},{6,5},{7,6},{9,8},{10,9},{11,10},{13,12},{... | collective-permute-start | bytes 1572872 | tf_op jit(solution)/shard_map/ppermute | solution.py:60
  247.2 2.0 copy-start.1
  249.7 16.6 %collective-permute-start = (f32[4,2,64,256]{3,2,1,0:T(8,128)S(1)}, f32[4,2,64,256]{3,2,1,0:T(8,128)S(1)}, u32[]{:S(2)}, u32[]{:S(2)}) collective-permute-start(f32[4,2,64,256]{3,2,1,0:T(8,128)S(1)} %multiply_add_fusion.14), channel_id=1, source_target_pairs={{1,0},{2,1},{3,2},{5,4},{6,5},{7,6},{9,8},{10,9},{11,10},{13,12},{... | collective-permute-start | bytes 1572872 | tf_op jit(solution)/shard_map/while/body/eval_jaxpr/ppermute | solution.py:60
  266.5 16.9 %collective-permute-start = (f32[4,2,64,256]{3,2,1,0:T(8,128)S(1)}, f32[4,2,64,256]{3,2,1,0:T(8,128)S(1)}, u32[]{:S(2)}, u32[]{:S(2)}) collective-permute-start(f32[4,2,64,256]{3,2,1,0:T(8,128)S(1)} %multiply_add_fusion.14), channel_id=1, source_target_pairs={{1,0},{2,1},{3,2},{5,4},{6,5},{7,6},{9,8},{10,9},{11,10},{13,12},{... | collective-permute-start | bytes 1572872 | tf_op jit(solution)/shard_map/while/body/eval_jaxpr/ppermute | solution.py:60
  283.4 15.7 %collective-permute-start = (f32[4,2,64,256]{3,2,1,0:T(8,128)S(1)}, f32[4,2,64,256]{3,2,1,0:T(8,128)S(1)}, u32[]{:S(2)}, u32[]{:S(2)}) collective-permute-start(f32[4,2,64,256]{3,2,1,0:T(8,128)S(1)} %multiply_add_fusion.14), channel_id=1, source_target_pairs={{1,0},{2,1},{3,2},{5,4},{6,5},{7,6},{9,8},{10,9},{11,10},{13,12},{... | collective-permute-start | bytes 1572872 | tf_op jit(solution)/shard_map/while/body/eval_jaxpr/ppermute | solution.py:60
  299.2 3.4 %copy-start.2 = (f32[8,4,2,64,256]{4,3,2,1,0:T(8,128)S(1)}, f32[8,4,2,64,256]{4,3,2,1,0:T(8,128)}, u32[]{:S(2)}) copy-start(f32[8,4,2,64,256]{4,3,2,1,0:T(8,128)} %copy-done.1) | copy-start | bytes 12582916
  303.0 2.0 copy-start.6
